TPU v7x, 256 devices: a whole 4x4x8 slice. The times are simulated.
256 devices in a mesh: tok: 16 (over y, x), voc: 8 (over z), hid: 2 (over core).
Axes of the slice: x: 4, y: 4, z: 8, core: 2. Of those that a mesh axis runs over, the one named last changes fastest.
Arguments:
- hidden: bfloat16 [2048, 4096], P('tok', 'hid')
- head_weight: bfloat16 [16000, 4096], P(('tok', 'voc'), 'hid')
- target_logits: bfloat16 [2048, 128256], P('tok', ('voc', 'hid'))
- vocab_order: int32 [128256], P(('voc', 'hid')), may hold values from 0 to 128255, as said below
- draft_map: int32 [16000], replicated, may hold values from 0 to 128255, as said below
- token_weight: float32 [2048], P('tok'), may hold values from 4 to 40
Outputs:
- token_kl: float32 [2048], P(('tok', 'hid'))
- grad_hidden: bfloat16 [2048, 4096], P(('tok', 'voc'), 'hid')
- grad_weight: bfloat16 [16000, 4096], P(('tok', 'voc'), 'hid')
Inputs may be any that keep to these rules, and one draw needn't show every extreme that they name: A permutation of the target ids: storage column j of target_logits holds the logit of target id vocab_order[j]. `draft_map`: 16000 distinct target ids. Draft id k belongs to voc index (k // 125) % 8. Among the 8016 storage columns of any one device of voc+hid, at most 250 hold the target ids of draft ids that belong to one voc index, and in every draw some device holds exactly 250 for some voc index.
All inputs are finite; a program needn't handle non-finite values.
Results may differ from a plain program's by a relative error of at most 0.018.
Values may be sent and summed in bfloat16 or wider, within the bound.
A program may use at most 64 MiB of HBM per device.

v0:
```python
import jax
import jax.numpy as jnp
from jax import lax
from jax.experimental import pallas as pl
from jax.experimental.pallas import tpu as pltpu
from jax.sharding import PartitionSpec as P

F32, BF16, I32 = jnp.float32, jnp.bfloat16, jnp.int32
MESH = pl.DeviceIdType.MESH
LOWEST = float(jnp.finfo(jnp.float32).min)
NT = (((1,), (1,)), ((), ()))
COLS = 8016
BLK = 125
D2 = 2048
Z_ORDER = (4, 3, 5, 2, 6, 1, 7, 0)
STEP = 256
PASS_ON = 4
PAIRS = D2 // STEP // 2
LAST = 2 * PAIRS - 1
VMEM_LIMIT = 48 * 1024 * 1024


def iota(shape, dim):
    return lax.broadcasted_iota(I32, shape, dim)


def low_lanes(shape):
    return iota(shape, 1) < 64


def swap(a):
    return pltpu.roll(a, 64, 1)


def kernel(
    ids_ref, order_ref, logits_ref, hidden_ref, weight_ref, row_weight_ref,
    kl_ref, gh_ref, gw_ref,
    row_weight_own, weight, logits, loc, slot, locz, used, slot_send, slot_recv, src_v, src_s, logits_t, picked, pick_send, pick_recv,
    idx_v, idx_s, rows, placed, x_send, x_recv, target, hid_all, w_all, d_own, d_send, d_recv,
    stat_x, stat_z, t_c, t_z, t_x, c_x, c_z, grad, grad_t, xs, ys, x_mid, y_mid, x_fin, y_fin, z_send, z_recv, zf_send, zf_recv, xf_send, xf_recv,
    loc_sem, ag_s, ag_r, copy_sem, src_sem, si_s, si_r, pk_s, pk_r, xa_s, xa_r, dd, sx_s, sx_r, sz_s, sz_r,
    tc, tz_s, tz_r, tx_s, tx_r, cx_s, cx_r, cz_s, cz_r, gg,
    rx_s, rx_r, ry_s, ry_r, rz_s, rz_r,
    zf_s, zf_r, xf_s, xf_r,
):
    tok, z, c = lax.axis_index("tok"), lax.axis_index("voc"), lax.axis_index("hid")
    y, x = tok // 4, tok % 4
    shard = z * 2 + c

    def x_peer(d):
        return (y * 4 + (x + d) % 4, z, c)

    def y_peer(d):
        return ((y + d) % 4 * 4 + x, z, c)

    def tok_peer(d):
        return ((tok + d) % 16, z, c)

    def voc_peer(dz, dc):
        return (tok, (z + dz) % 8, (c + dc) % 2)

    unsent, unreceived = [], []

    def send(src, dst, ssem, rsem, peer):
        copy = pltpu.make_async_remote_copy(
            src_ref=src, dst_ref=dst, send_sem=ssem, recv_sem=rsem, device_id=peer, device_id_type=MESH
        )
        copy.start()
        unsent.append(copy)
        unreceived.append(copy)
        return copy

    def arrive(copies):
        for copy in copies:
            copy.wait_recv()
            unreceived[:] = [other for other in unreceived if other is not copy]

    def drain():
        arrive(list(unreceived))
        for copy in unsent:
            copy.wait_send()

    voc_pairs = [(dz, dc) for dz in Z_ORDER for dc in (0, 1) if dz or dc]

    barrier = pltpu.get_barrier_semaphore()
    for d in range(1, 16):
        pl.semaphore_signal(barrier, inc=1, device_id=tok_peer(d), device_id_type=MESH)
    for dz, dc in voc_pairs:
        pl.semaphore_signal(barrier, inc=1, device_id=voc_peer(dz, dc), device_id_type=MESH)

    logits_in = pltpu.make_async_copy(logits_ref, logits, copy_sem.at[0])
    hidden_in = pltpu.make_async_copy(hidden_ref, hid_all.at[:, x], copy_sem.at[1])
    weight_in = pltpu.make_async_copy(weight_ref, weight, copy_sem.at[2])
    row_weight_in = pltpu.make_async_copy(row_weight_ref, row_weight_own, copy_sem.at[3])
    for copy in (weight_in, hidden_in, logits_in, row_weight_in):
        copy.start()

    lane = iota((128, 128), 1)
    ids_t = jnp.concatenate([ids_ref[...], jnp.zeros((120, 128), I32)], axis=0).T
    best = jnp.zeros((128, 128), F32)
    for zz in range(8):
        wanted = jnp.broadcast_to(ids_t[:, zz : zz + 1], (128, 128))

        def step(b, acc, wanted=wanted):
            return jnp.where(order_ref[pl.ds(b, 1), :] == wanted, b, acc)

        acc = lax.fori_loop(0, 63, step, jnp.full((128, 128), -1, I32), unroll=9)
        found = jnp.where(acc >= 0, acc * 128 + lane, -1).astype(F32)
        best = jnp.where(lane == zz, jnp.max(found, axis=1, keepdims=True), best)
    loc[tok] = best.T[:8].astype(I32)

    pl.semaphore_wait(barrier, 30)
    loc_copies = [
        send(loc.at[tok], loc.at[tok], loc_sem.at[0, d], loc_sem.at[1, d], tok_peer(d)) for d in range(1, 16)
    ]

    weight_in.wait()
    w_all[y, 0] = weight[:64, :]
    w_all[y, 1] = jnp.concatenate([weight[64:, :], jnp.zeros((128 - BLK, D2), BF16)], axis=0)

    def spread(source, first, peer, base):
        copies = []
        for k, (h, d) in enumerate(((0, 1), (1, -1), (1, 1), (0, -1))):
            copies.append(send(source.at[h], first(h, 0), ag_s.at[base + k], ag_r.at[base + k], peer(d)))
        return copies

    def hid_at(h, d):
        return hid_all.at[h, (x + d) % 4]

    def w_at(h, d):
        return w_all.at[(y + d) % 4, h]

    hid_copies = spread(hidden_ref, hid_at, x_peer, 0)
    w_copies = spread(w_all.at[y], w_at, y_peer, 6)

    logits_in.wait()

    def widen(b, _):
        part = pl.ds(pl.multiple_of(b * 48, 48), 48)
        logits_t[part, :] = logits[part, :].astype(F32)
        return 0

    lax.fori_loop(0, COLS // 48, widen, 0, unroll=4)

    arrive(loc_copies)

    r0, r1 = iota((128, 128), 0), iota((128, 128), 1)
    before = (r0 < r1).astype(BF16)
    earlier = ((r0 & 7 == (r1 & 7)) & (r1 >> 3 < r0 >> 3)).astype(BF16)
    place = loc[...].reshape(128, 128).astype(F32)
    held = place >= 0.0
    held_b = held.astype(F32).astype(BF16)
    in_row = jnp.dot(held_b, before, preferred_element_type=F32)
    count = jnp.dot(held_b, jnp.ones((128, 128), BF16), preferred_element_type=F32)
    rank = in_row + jnp.dot(earlier, count.astype(BF16), preferred_element_type=F32)
    slot[...] = jnp.where(held, rank, -1.0)
    locz[...] = place
    same = (r0 & 7 == (r1 & 7)).astype(BF16)
    used[...] = jnp.dot(same, count.astype(BF16), preferred_element_type=F32)[:8]
    for zz in range(8):
        slot_send[zz] = slot[pl.ds(zz, 16, stride=8), :].astype(BF16)
    slot_recv[shard] = slot_send[z]

    def list_slots(k):
        zz = (z + Z_ORDER[k]) % 8
        columns = []
        for half in range(2):
            mine = (iota((128, 128), 0) + half * 128).astype(F32)

            def step(t, acc, mine=mine):
                row = pl.ds(t * 8 + zz, 1)
                return jnp.where(slot[row, :] == mine, locz[row, :], acc)

            acc = lax.fori_loop(0, 16, step, jnp.zeros((128, 128), F32), unroll=8)
            columns.append(jnp.sum(acc.T, axis=0, keepdims=True))
        column = jnp.clip(jnp.concatenate(columns, axis=1).astype(I32), 0, COLS - 1)
        src_v[k] = jnp.broadcast_to(column, (8, 256))
        copy = pltpu.make_async_copy(src_v.at[k], src_s.at[k], src_sem.at[k])
        copy.start()
        return copy

    listed = list_slots(0)

    def pass_on(copies, at, peer, base):
        out = []
        for k, d in ((0, -1), (1, 1)):
            arrive([copies[k]])
            out.append(send(at(k, d), at(k, d), ag_s.at[base + 4 + k], ag_r.at[base + 4 + k], peer(-d)))
        return out

    lanes = low_lanes((128, 128))
    pick_copies, slot_copies = [], []
    for k, dz in enumerate(Z_ORDER):
        zz = (z + dz) % 8
        following = list_slots(k + 1) if k < 7 else None
        listed.wait()
        listed = following

        if k == PASS_ON:
            hidden_in.wait()
            hid_more = pass_on(hid_copies, hid_at, x_peer, 0)
            w_more = pass_on(w_copies, w_at, y_peer, 6)
        def pick(g, _, zz=zz, k=k):
            for i in range(16):
                s = g * 16 + i
                picked[zz, pl.ds(s, 1), :] = logits_t[pl.ds(src_s[k, 0, s], 1), :]
            return 0

        lax.fori_loop(0, 16, pick, 0)
        first, second = picked[zz, :128, :], picked[zz, 128:, :]
        pick_send[zz, 0] = jnp.where(lanes, first, swap(second)).astype(BF16)
        pick_send[zz, 1] = jnp.where(lanes, swap(first), second).astype(BF16)
        for dc in (0, 1):
            if dz or dc:
                pick_copies.append(
                    send(
                        pick_send.at[zz, (c + dc) % 2], pick_recv.at[shard],
                        pk_s.at[dz * 2 + dc], pk_r.at[dz * 2 + dc], voc_peer(dz, dc),
                    )
                )
        if k == 1:
            slot_copies = [
                send(
                    slot_send.at[(z + ez) % 8], slot_recv.at[shard],
                    si_s.at[ez * 2 + ec], si_r.at[ez * 2 + ec], voc_peer(ez, ec),
                )
                for ez, ec in voc_pairs
            ]
    pick_recv[shard] = pick_send[z, c]

    def packed(stats):
        width = stats[0].shape[1]
        return jnp.concatenate(list(stats) + [jnp.zeros((8 - len(stats), width), F32)], axis=0)

    def merge(ref, n, row=0):
        part = [ref[i][row : row + 2] for i in range(n)]
        top = part[0][0:1]
        for p in part[1:]:
            top = jnp.maximum(top, p[0:1])
        return top, sum(p[1:2] * jnp.exp(p[0:1] - top) for p in part)

    def to_x(ref, ss, rr):
        return [send(ref.at[x], ref.at[x], ss.at[d], rr.at[d], x_peer(d)) for d in (2, 1, 3)]

    def to_z(ref, ss, rr):
        return [send(ref.at[z], ref.at[z], ss.at[d], rr.at[d], voc_peer(d, 0)) for d in Z_ORDER[:-1]]

    slots_used = used[...]
    seen = picked[...]
    valid = iota((8, 256, 128), 1).astype(F32) < slots_used.reshape(8, 1, 128)
    top_t = jnp.max(jnp.where(valid, seen, LOWEST), axis=(0, 1), keepdims=True)[0]
    sum_t = jnp.sum(jnp.where(valid, jnp.exp(seen - top_t[None]), 0.0), axis=(0, 1), keepdims=True)[0]
    t_c[c] = packed((top_t, sum_t))
    t_copy = send(t_c.at[c], t_c.at[c], tc.at[0], tc.at[1], voc_peer(0, 1))

    arrive(slot_copies)
    index = jnp.zeros((16, 128), F32)
    for s in range(16):
        got = slot_recv[s].astype(F32)
        index = jnp.where(got >= 0.0, got + s * 256.0, index)
    idx_v[...] = jnp.clip(index.astype(I32), 0, 4095)
    to_smem = pltpu.make_async_copy(idx_v, idx_s, copy_sem.at[4])
    to_smem.start()
    to_smem.wait()

    arrive([t_copy])
    t_z[z] = packed(merge(t_c, 2))
    t_copies = to_z(t_z, tz_s, tz_r)

    arrive(hid_copies[2:] + w_copies[2:] + hid_more + w_more)

    def partial_draft(core, out):
        tokens = hid_all[core].reshape(256, D2)

        def step(i, _):
            part = w_all[pl.ds(i * 2, 2)].reshape(256, D2)
            out[pl.ds(pl.multiple_of(i * 256, 256), 256), :] = lax.dot_general(
                part, tokens, NT, preferred_element_type=F32
            )
            return 0

        lax.fori_loop(0, 2, step, 0)

    partial_draft(1 - c, d_send)
    d_copy = send(d_send, d_recv, dd.at[0], dd.at[1], voc_peer(0, 1))
    partial_draft(c, d_own)

    arrive([d_copy])
    real = (iota((512, 256), 0) & 127) < BLK
    draft_l = d_own[...] + d_recv[...]
    d_own[...] = draft_l
    top_d = jnp.max(jnp.where(real, draft_l, -jnp.inf), axis=0, keepdims=True)
    sum_d = jnp.sum(jnp.where(real, jnp.exp(draft_l - top_d), 0.0), axis=0, keepdims=True)
    row_weight_in.wait()
    weights = row_weight_own[...]
    weights = jnp.where(low_lanes((1, 128)) == (c == 0), weights, swap(weights))
    weights = jnp.where(iota((1, 256), 1) >> 6 == x, jnp.concatenate([weights, weights], axis=1), 0.0)
    stat_x[x] = packed((top_d, sum_d, weights))
    d_copies = to_x(stat_x, sx_s, sx_r)

    arrive(pick_copies)

    def unpack(s, _):
        block = pick_recv[s].astype(F32)
        rows[pl.ds(pl.multiple_of(s * 256, 256), 128), :] = block
        rows[pl.ds(pl.multiple_of(s * 256 + 128, 128), 128), :] = swap(block)
        return 0

    lax.fori_loop(0, 16, unpack, 0)

    x_copies = []
    for d in (2, 1, 3, 0):
        xx = (x + d) % 4

        def place_rows(i, _, xx=xx):
            t = (i >> 3) * 4 + xx
            for k in range(16):
                r = (i & 7) * 16 + k
                placed[t, pl.ds(r, 1), :] = rows[pl.ds(idx_s[t, r], 1), :]
            return 0

        lax.fori_loop(0, 32, place_rows, 0)
        for k in range(2):
            x_send[xx, k * 128 : k * 128 + 128, :] = jnp.where(
                lanes, placed[k * 4 + xx], swap(placed[k * 4 + 8 + xx])
            ).astype(BF16)
        if d:
            x_copies.append(send(x_send.at[xx], x_recv.at[x], xa_s.at[d], xa_r.at[d], x_peer(d)))
    x_recv[x] = x_send[x]

    arrive(t_copies)
    top_t, sum_t = merge(t_z, 8)
    t_x[x] = packed((top_t + jnp.log(sum_t),))
    t_copies = to_x(t_x, tx_s, tx_r)
    arrive(d_copies)
    row_weight = stat_x[0][2:3] + stat_x[1][2:3] + stat_x[2][2:3] + stat_x[3][2:3]
    stat_z[z] = packed(merge(stat_x, 4))
    d_copies = to_z(stat_z, sz_s, sz_r)

    arrive(x_copies)
    lanes2 = low_lanes((256, 128))
    for j in range(2):
        first, second = x_recv[2 * j].astype(F32), x_recv[2 * j + 1].astype(F32)
        target[:256, j * 128 : j * 128 + 128] = jnp.where(lanes2, first, swap(second))
        target[256:, j * 128 : j * 128 + 128] = jnp.where(lanes2, swap(first), second)
    arrive(t_copies)
    lanes1 = low_lanes((1, 128))

    def pair_up(first, second):
        return jnp.where(lanes1, jnp.where(c == 0, first, swap(first)), jnp.where(c == 0, swap(second), second))

    norm_t = jnp.concatenate(
        [pair_up(t_x[2 * j][0:1], t_x[2 * j + 1][0:1]) for j in range(2)], axis=1
    )

    arrive(d_copies)
    top_d, sum_d = merge(stat_z, 8)
    norm_d = top_d + jnp.log(sum_d)

    probs = jnp.exp(target[...] - norm_t)
    grad_l = row_weight * (jnp.exp(d_own[...] - norm_d) - probs)
    grad_l = jnp.where(real, grad_l, 0.0)
    grad[c] = grad_l.astype(BF16)
    g_copy = send(grad.at[c], grad.at[c], gg.at[0], gg.at[1], voc_peer(0, 1))
    grad_t[c] = grad_l.T.astype(BF16).reshape(4, 64, 512)
    cross = jnp.sum(jnp.where(real, probs * (target[...] - d_own[...]), 0.0), axis=0, keepdims=True)
    c_x[x] = packed((cross,))
    cross_copies = to_x(c_x, cx_s, cx_r)
    arrive([g_copy])
    grad_t[1 - c] = grad[1 - c].astype(F32).T.astype(BF16).reshape(4, 64, 512)

    def ring(buf, mid, fin, me, peer, ss, rr):
        def remote(kind, p, block, dst, d):
            return pltpu.make_async_remote_copy(
                src_ref=buf.at[p, (me + block + 4) % 4], dst_ref=dst, send_sem=ss.at[kind, p],
                recv_sem=rr.at[kind, p], device_id=peer(d), device_id_type=MESH,
            )

        def copies(p, h):
            d = 1 - 2 * h
            return (
                remote(0, p, 2, mid.at[p], d),
                remote(1, p, -d, fin.at[p, 1 - h], -d),
                remote(2, p, d, fin.at[p, h], d),
            )

        def early(p, h):
            copies(p, h)[0].start()

        def late(p, h):
            far, near, summed = copies(p, h)
            near.start()
            far.wait_recv()
            block = (me + 1 - 2 * h + 4) % 4
            buf[p, block] = (buf[p, block].astype(F32) + mid[p].astype(F32)).astype(BF16)
            summed.start()

        def total(p, h):
            _, near, summed = copies(p, h)
            near.wait_recv()
            summed.wait_recv()
            return buf[p, me].astype(F32) + fin[p, 0].astype(F32) + fin[p, 1].astype(F32)

        def sent(p, h):
            for copy in copies(p, h):
                copy.wait_send()

        return early, late, total, sent

    x_early, x_late, x_total, x_sent = ring(xs, x_mid, x_fin, x, x_peer, rx_s, rx_r)
    y_early, y_late, y_total, y_sent = ring(ys, y_mid, y_fin, y, y_peer, ry_s, ry_r)

    def columns(p):
        return pl.ds(pl.multiple_of(p * STEP, STEP), STEP)

    def hidden_product(p):
        right = w_all[:, :, :, columns(p)].reshape(512, STEP)
        out = jnp.dot(grad_t[...].reshape(512, 512), right, preferred_element_type=F32)
        return out.astype(BF16).reshape(2, 4, 64, STEP)

    def hidden_piece(p):
        out = hidden_product(p)
        for a in range(2):
            for b in range(4):
                xs[p, b, a * 64 : a * 64 + 64, :] = out[a, b]

    def weight_piece(p):
        right = hid_all[:, :, :, columns(p)].reshape(2, 256, STEP)
        out = jnp.dot(grad[0], right[0], preferred_element_type=F32)
        out += jnp.dot(grad[1], right[1], preferred_element_type=F32)
        ys[p] = out.astype(BF16).reshape(4, 128, STEP)

    def z_copy(i, d, *part):
        return pltpu.make_async_remote_copy(
            src_ref=z_send.at[(i, (z + d) % 8, *part)], dst_ref=z_recv.at[(i, z, *part)],
            send_sem=rz_s.at[i, d], recv_sem=rz_r.at[i, d], device_id=voc_peer(d, 0), device_id_type=MESH,
        )

    out = hidden_product(LAST)
    for a in range(2):
        for k in range(4):
            for b in range(4):
                zf_send[a * 4 + k, b] = out[a, b, k * 16 : k * 16 + 16]
    zf_copies = [
        send(zf_send.at[(z + d) % 8], zf_recv.at[z], zf_s.at[d], zf_r.at[d], voc_peer(d, 0)) for d in Z_ORDER[:-1]
    ]
    zf_recv[z] = zf_send[z]

    def x_pieces(i, work):
        work(2 * i, 0)
        pl.when(i < PAIRS - 1)(lambda: work(2 * i + 1, 1))

    def turn(i, _):
        @pl.when(i < PAIRS)
        def _():
            def product(p, h):
                hidden_piece(p)
                x_early(p, h)

            x_pieces(i, product)
            for h in range(2):
                weight_piece(2 * i + h)
                y_early(2 * i + h, h)

        @pl.when((i >= 1) & (i < PAIRS + 1))
        def _():
            x_pieces(i - 1, x_late)
            for h in range(2):
                y_late(2 * i - 2 + h, h)

        @pl.when(i >= 2)
        def _():
            pair = i - 2

            def total(p, h):
                z_send[pair, :, h] = x_total(p, h).astype(BF16).reshape(8, 16, STEP)

            x_pieces(pair, total)

            @pl.when(pair < PAIRS - 1)
            def _():
                for d in Z_ORDER[:-1]:
                    z_copy(pair, d).start()
                z_recv[pair, z, 1] = z_send[pair, z, 1]

            @pl.when(pair == PAIRS - 1)
            def _():
                for d in Z_ORDER[:-1]:
                    z_copy(pair, d, 0).start()

            z_recv[pair, z, 0] = z_send[pair, z, 0]
            for h in range(2):
                gw_ref[:, columns(2 * pair + h)] = y_total(2 * pair + h, h).astype(BF16)

        return 0

    lax.fori_loop(0, 3, turn, 0)
    arrive(zf_copies)
    out = zf_recv[0].astype(F32)
    for k in range(1, 8):
        out += zf_recv[k].astype(F32)
    xf_send[...] = out.astype(BF16)
    xf_copies = [
        send(xf_send.at[(x + d) % 4], xf_recv.at[x], xf_s.at[d], xf_r.at[d], x_peer(d)) for d in (2, 1, 3)
    ]
    xf_recv[x] = xf_send[x]
    lax.fori_loop(3, PAIRS + 2, turn, 0)
    arrive(cross_copies)
    c_z[z] = c_x[0] + c_x[1] + c_x[2] + c_x[3]
    cross_copies = to_z(c_z, cz_s, cz_r)

    def summed(i, h):
        out = z_recv[i, 0, h].astype(F32)
        for k in range(1, 8):
            out += z_recv[i, k, h].astype(F32)
        gh_ref[:, columns(2 * i + h)] = out.astype(BF16)

    arrive(xf_copies)
    gh_ref[:, LAST * STEP :] = sum(xf_recv[k].astype(F32) for k in range(4)).astype(BF16)

    def finish(i, _):
        @pl.when(i < PAIRS - 1)
        def _():
            for d in Z_ORDER[:-1]:
                z_copy(i, d).wait()
            summed(i, 1)

        @pl.when(i == PAIRS - 1)
        def _():
            for d in Z_ORDER[:-1]:
                z_copy(i, d, 0).wait()

        summed(i, 0)
        x_pieces(i, x_sent)
        for h in range(2):
            y_sent(2 * i + h, h)
        return 0

    lax.fori_loop(0, PAIRS, finish, 0)
    arrive(cross_copies)
    cross = sum(c_z[i][0:1] for i in range(8))
    kl = cross - norm_t + norm_d
    kl = jnp.where(x < 2, kl[:, :128], kl[:, 128:])
    kl_ref[...] = jnp.where(x % 2 == 0, kl, swap(kl))
    drain()


def body(hidden, head_weight, target_logits, vocab_order, draft_map, token_weight):
    tok = lax.axis_index("tok")
    ids = lax.dynamic_slice_in_dim(draft_map, tok * 8 * BLK, 8 * BLK, 0).reshape(8, BLK)
    ids = jnp.pad(ids, ((0, 0), (0, 128 - BLK)), constant_values=-2)
    order = jnp.pad(vocab_order, (0, 63 * 128 - COLS), constant_values=-1).reshape(63, 128)
    in_place = (target_logits.T, hidden.reshape(2, 64, D2), head_weight, token_weight.reshape(1, 128))

    vmem = pl.BlockSpec(memory_space=pltpu.VMEM)
    hbm = pl.BlockSpec(memory_space=pltpu.HBM)
    dma = pltpu.SemaphoreType.DMA
    scratch = [
        pltpu.VMEM((1, 128), F32),
        pltpu.VMEM((BLK, D2), BF16),
        pltpu.VMEM((COLS, 128), BF16),
        pltpu.VMEM((16, 8, 128), I32),
        pltpu.VMEM((128, 128), F32),
        pltpu.VMEM((128, 128), F32),
        pltpu.VMEM((8, 128), F32),
        pltpu.VMEM((8, 16, 128), BF16),
        pltpu.VMEM((16, 16, 128), BF16),
        pltpu.VMEM((8, 8, 256), I32),
        pltpu.SMEM((8, 8, 256), I32),
        pltpu.VMEM((COLS, 128), F32),
        pltpu.VMEM((8, 256, 128), F32),
        pltpu.VMEM((8, 2, 128, 128), BF16),
        pltpu.VMEM((16, 128, 128), BF16),
        pltpu.VMEM((16, 128), I32),
        pltpu.SMEM((16, 128), I32),
        pltpu.VMEM((4096, 128), F32),
        pltpu.VMEM((16, 128, 128), F32),
        pltpu.VMEM((4, 256, 128), BF16),
        pltpu.VMEM((4, 256, 128), BF16),
        pltpu.VMEM((512, 256), F32),
        pltpu.VMEM((2, 4, 64, D2), BF16),
        pltpu.VMEM((4, 2, 64, D2), BF16),
        pltpu.VMEM((512, 256), F32),
        pltpu.VMEM((512, 256), F32),
        pltpu.VMEM((512, 256), F32),
        pltpu.VMEM((4, 8, 256), F32),
        pltpu.VMEM((8, 8, 256), F32),
        pltpu.VMEM((2, 8, 128), F32),
        pltpu.VMEM((8, 8, 128), F32),
        pltpu.VMEM((4, 8, 128), F32),
        pltpu.VMEM((4, 8, 256), F32),
        pltpu.VMEM((8, 8, 256), F32),
        pltpu.VMEM((2, 512, 256), BF16),
        pltpu.VMEM((2, 4, 64, 512), BF16),
        pltpu.VMEM((2 * PAIRS, 4, 128, STEP), BF16),
        pltpu.VMEM((2 * PAIRS, 4, 128, STEP), BF16),
        pltpu.VMEM((2 * PAIRS, 128, STEP), BF16),
        pltpu.VMEM((2 * PAIRS, 128, STEP), BF16),
        pltpu.VMEM((2 * PAIRS, 2, 128, STEP), BF16),
        pltpu.VMEM((2 * PAIRS, 2, 128, STEP), BF16),
        pltpu.VMEM((PAIRS, 8, 2, 16, STEP), BF16),
        pltpu.VMEM((PAIRS, 8, 2, 16, STEP), BF16),
        pltpu.VMEM((8, 4, 16, STEP), BF16),
        pltpu.VMEM((8, 4, 16, STEP), BF16),
        pltpu.VMEM((4, 16, STEP), BF16),
        pltpu.VMEM((4, 16, STEP), BF16),
        dma((2, 16)),
        dma((12,)), dma((12,)),
        dma((5,)),
        dma((8,)),
        dma((16,)), dma((16,)),
        dma((16,)), dma((16,)),
        dma((4,)), dma((4,)),
        dma((2,)),
        dma((4,)), dma((4,)),
        dma((8,)), dma((8,)),
        dma((2,)),
        dma((8,)), dma((8,)),
        dma((4,)), dma((4,)),
        dma((4,)), dma((4,)),
        dma((8,)), dma((8,)),
        dma((2,)),
        dma((3, 2 * PAIRS)), dma((3, 2 * PAIRS)),
        dma((3, 2 * PAIRS)), dma((3, 2 * PAIRS)),
        dma((PAIRS, 8)), dma((PAIRS, 8)),
        dma((8,)), dma((8,)),
        dma((4,)), dma((4,)),
    ]
    kl, grad_hidden, grad_weight = pl.pallas_call(
        kernel,
        out_shape=(
            jax.ShapeDtypeStruct((1, 128), F32),
            jax.ShapeDtypeStruct((16, D2), BF16),
            jax.ShapeDtypeStruct((128, D2), BF16),
        ),
        in_specs=[vmem, vmem, hbm, hbm, hbm, hbm],
        out_specs=(vmem, vmem, vmem),
        scratch_shapes=scratch,
        compiler_params=pltpu.CompilerParams(
            collective_id=0, has_side_effects=True, vmem_limit_bytes=VMEM_LIMIT
        ),
        name="draft_head",
    )(ids, order, *(pltpu.with_memory_space_constraint(a, pltpu.HBM) for a in in_place))
    return kl[0, :64], grad_hidden, grad_weight[:BLK]


def solution(mesh):
    placed = (
        P("tok", "hid"),
        P(("tok", "voc"), "hid"),
        P("tok", ("voc", "hid")),
        P(("voc", "hid")),
        P(),
        P("tok"),
    )
    return jax.shard_map(
        body,
        mesh=mesh,
        in_specs=placed,
        out_specs=(P(("tok", "hid")), P(("tok", "voc"), "hid"), P(("tok", "voc"), "hid")),
        check_vma=False,
    )
```

profile of v0, /device:TPU:1, one launch (start us, length us, event | category | flops | bytes accessed | tf_op | source)
XLA Modules:
  0.0 79.6 jit_solution(962519858299608676)
XLA Ops:
  0.6 0.8 dynamic_slice.3
  1.4 0.1 reshape.18
  1.5 0.8 pad_bitcast_fusion.order_ref
  2.3 75.4 %draft_head.1 = (f32[1,128]{1,0:T(1,128)S(1)}, bf16[16,2048]{1,0:T(8,128)(2,1)S(1)}, bf16[128,2048]{1,0:T(8,128)(2,1)S(1)}) custom-call(s32[8,128]{1,0:T(8,128)S(1)} %pad.8.ids_ref, s32[63,128]{1,0:T(8,128)S(1)} %pad_bitcast_fusion.order_ref, bf16[8016,128]{1,0:T(8,128)(2,1)} %bitcast.9, bf16[2,64,2048]{2,1,0:T(8,128)(2,1)} %bitcast.10, ...), custom_call_target="tpu_custom_call" | custom-call | tf_op jit(solution)/shard_map/draft_head/pallas_call | solution.py:629
  77.7 0.5 slice_bitcast_fusion
  78.2 0.6 copy.11
  78.8 0.8 copy.12
  (1 shorter events, 0.0 us)
where the time goes:
time: 79.8 us; the launch traced here: 79.6 us
  Pallas kernels  75.4 us (94%)
  local copies, waits for them, and re-layouts  3.56 us (4%)
    pallas_call x1, Pallas kernels, body(): pl.pallas_call(kernel, out_shape=(jax.ShapeDtypeStruct((1, 128), F32), ja...  75.4 us

commit v1 on v0

--- a/solution.py
+++ b/solution.py
@@ -436,15 +436,38 @@
             send_sem=rz_s.at[i, d], recv_sem=rz_r.at[i, d], device_id=voc_peer(d, 0), device_id_type=MESH,
         )
 
-    out = hidden_product(LAST)
-    for a in range(2):
-        for k in range(4):
-            for b in range(4):
-                zf_send[a * 4 + k, b] = out[a, b, k * 16 : k * 16 + 16]
-    zf_copies = [
-        send(zf_send.at[(z + d) % 8], zf_recv.at[z], zf_s.at[d], zf_r.at[d], voc_peer(d, 0)) for d in Z_ORDER[:-1]
-    ]
-    zf_recv[z] = zf_send[z]
+    def zf_copy(d):
+        return pltpu.make_async_remote_copy(
+            src_ref=zf_send.at[(z + d) % 8], dst_ref=zf_recv.at[z], send_sem=zf_s.at[d], recv_sem=zf_r.at[d],
+            device_id=voc_peer(d, 0), device_id_type=MESH,
+        )
+
+    def xf_copy(d):
+        return pltpu.make_async_remote_copy(
+            src_ref=xf_send.at[(x + d) % 4], dst_ref=xf_recv.at[x], send_sem=xf_s.at[d], recv_sem=xf_r.at[d],
+            device_id=x_peer(d), device_id_type=MESH,
+        )
+
+    def z_first():
+        out = hidden_product(LAST)
+        for a in range(2):
+            for k in range(4):
+                for b in range(4):
+                    zf_send[a * 4 + k, b] = out[a, b, k * 16 : k * 16 + 16]
+        for d in Z_ORDER[:-1]:
+            zf_copy(d).start()
+        zf_recv[z] = zf_send[z]
+
+    def x_second():
+        for d in Z_ORDER[:-1]:
+            zf_copy(d).wait()
+        out = zf_recv[0].astype(F32)
+        for k in range(1, 8):
+            out += zf_recv[k].astype(F32)
+        xf_send[...] = out.astype(BF16)
+        for d in (2, 1, 3):
+            xf_copy(d).start()
+        xf_recv[x] = xf_send[x]
 
     def x_pieces(i, work):
         work(2 * i, 0)
@@ -462,6 +485,9 @@
                 weight_piece(2 * i + h)
                 y_early(2 * i + h, h)
 
+        pl.when(i == 0)(z_first)
+        pl.when(i == 3)(x_second)
+
         @pl.when((i >= 1) & (i < PAIRS + 1))
         def _():
             x_pieces(i - 1, x_late)
@@ -494,17 +520,7 @@
 
         return 0
 
-    lax.fori_loop(0, 3, turn, 0)
-    arrive(zf_copies)
-    out = zf_recv[0].astype(F32)
-    for k in range(1, 8):
-        out += zf_recv[k].astype(F32)
-    xf_send[...] = out.astype(BF16)
-    xf_copies = [
-        send(xf_send.at[(x + d) % 4], xf_recv.at[x], xf_s.at[d], xf_r.at[d], x_peer(d)) for d in (2, 1, 3)
-    ]
-    xf_recv[x] = xf_send[x]
-    lax.fori_loop(3, PAIRS + 2, turn, 0)
+    lax.fori_loop(0, PAIRS + 2, turn, 0)
     arrive(cross_copies)
     c_z[z] = c_x[0] + c_x[1] + c_x[2] + c_x[3]
     cross_copies = to_z(c_z, cz_s, cz_r)
@@ -515,7 +531,8 @@
             out += z_recv[i, k, h].astype(F32)
         gh_ref[:, columns(2 * i + h)] = out.astype(BF16)
 
-    arrive(xf_copies)
+    for d in (2, 1, 3):
+        xf_copy(d).wait()
     gh_ref[:, LAST * STEP :] = sum(xf_recv[k].astype(F32) for k in range(4)).astype(BF16)
 
     def finish(i, _):

time: 79.8 us -> 79.8 us (level)
  no operation moved by 1% of the time
where the time goes in v1:
time: 79.8 us; the launch traced here: 79.7 us
  Pallas kernels  75.4 us (94%)
  local copies, waits for them, and re-layouts  3.56 us (4%)
    pallas_call x1, Pallas kernels, body(): pl.pallas_call(kernel, out_shape=(jax.ShapeDtypeStruct((1, 128), F32), ja...  75.4 us

profile of v1, /device:TPU:1, one launch (start us, length us, event | category | flops | bytes accessed | tf_op | source)
XLA Modules:
  0.0 79.7 jit_solution(9302212438352809703)
XLA Ops:
  0.6 0.8 dynamic_slice.3
  1.4 0.1 reshape.18
  1.5 0.8 pad_bitcast_fusion.order_ref
  2.3 75.4 %draft_head.1 = (f32[1,128]{1,0:T(1,128)S(1)}, bf16[16,2048]{1,0:T(8,128)(2,1)S(1)}, bf16[128,2048]{1,0:T(8,128)(2,1)S(1)}) custom-call(s32[8,128]{1,0:T(8,128)S(1)} %pad.8.ids_ref, s32[63,128]{1,0:T(8,128)S(1)} %pad_bitcast_fusion.order_ref, bf16[8016,128]{1,0:T(8,128)(2,1)} %bitcast.9, bf16[2,64,2048]{2,1,0:T(8,128)(2,1)} %bitcast.10, ...), custom_call_target="tpu_custom_call" | custom-call | tf_op jit(solution)/shard_map/draft_head/pallas_call | solution.py:646
  77.7 0.5 slice_bitcast_fusion
  78.2 0.6 copy.11
  78.9 0.8 copy.12
  (1 shorter events, 0.0 us)

commit v2 on v0

--- a/solution.py
+++ b/solution.py
@@ -14,6 +14,7 @@
 D2 = 2048
 Z_ORDER = (4, 3, 5, 2, 6, 1, 7, 0)
 STEP = 256
+FAR_FIRST = (10, 6, 9, 11, 14, 5, 7, 2, 8, 13, 15, 1, 3, 4, 12)
 PASS_ON = 4
 PAIRS = D2 // STEP // 2
 LAST = 2 * PAIRS - 1
@@ -111,7 +112,7 @@
 
     pl.semaphore_wait(barrier, 30)
     loc_copies = [
-        send(loc.at[tok], loc.at[tok], loc_sem.at[0, d], loc_sem.at[1, d], tok_peer(d)) for d in range(1, 16)
+        send(loc.at[tok], loc.at[tok], loc_sem.at[0, d], loc_sem.at[1, d], tok_peer(d)) for d in FAR_FIRST
     ]
 
     weight_in.wait()
@@ -298,15 +299,15 @@
     stat_x[x] = packed((top_d, sum_d, weights))
     d_copies = to_x(stat_x, sx_s, sx_r)
 
-    arrive(pick_copies)
-
-    def unpack(s, _):
+    def unpack(s):
         block = pick_recv[s].astype(F32)
         rows[pl.ds(pl.multiple_of(s * 256, 256), 128), :] = block
         rows[pl.ds(pl.multiple_of(s * 256 + 128, 128), 128), :] = swap(block)
-        return 0
-
-    lax.fori_loop(0, 16, unpack, 0)
+
+    unpack(shard)
+    for (dz, dc), copy in zip(voc_pairs, pick_copies):
+        arrive([copy])
+        unpack((z - dz + 8) % 8 * 2 + (c - dc + 2) % 2)
 
     x_copies = []
     for d in (2, 1, 3, 0):

time: 79.8 us -> 79.6 us (level)
  no operation moved by 1% of the time
where the time goes in v2:
time: 79.6 us; the launch traced here: 79.3 us
  Pallas kernels  75.1 us (94%)
  local copies, waits for them, and re-layouts  3.56 us (4%)
    pallas_call x1, Pallas kernels, body(): pl.pallas_call(kernel, out_shape=(jax.ShapeDtypeStruct((1, 128), F32), ja...  75.1 us

profile of v2, /device:TPU:1, one launch (start us, length us, event | category | flops | bytes accessed | tf_op | source)
XLA Modules:
  0.0 79.3 jit_solution(15472775186507493687)
XLA Ops:
  0.6 0.8 dynamic_slice.3
  1.4 0.1 reshape.18
  1.5 0.8 pad_bitcast_fusion.order_ref
  2.3 75.1 %draft_head.1 = (f32[1,128]{1,0:T(1,128)S(1)}, bf16[16,2048]{1,0:T(8,128)(2,1)S(1)}, bf16[128,2048]{1,0:T(8,128)(2,1)S(1)}) custom-call(s32[8,128]{1,0:T(8,128)S(1)} %pad.8.ids_ref, s32[63,128]{1,0:T(8,128)S(1)} %pad_bitcast_fusion.order_ref, bf16[8016,128]{1,0:T(8,128)(2,1)} %bitcast.9, bf16[2,64,2048]{2,1,0:T(8,128)(2,1)} %bitcast.10, ...), custom_call_target="tpu_custom_call" | custom-call | tf_op jit(solution)/shard_map/draft_head/pallas_call | solution.py:630
  77.4 0.5 slice_bitcast_fusion
  77.9 0.6 copy.11
  78.6 0.8 copy.12
  (1 shorter events, 0.0 us)
